TPU v7x, 128 devices: a whole 4x4x4 slice. The times are simulated.
128 devices in a mesh: dp: 4 (over y), fsdp: 32 (over z, x, core).
Axes of the slice: x: 4, y: 4, z: 4, core: 2. Of those that a mesh axis runs over, the one named last changes fastest.
Arguments:
- grad_parts: bfloat16 [4, 36, 1024, 1024], P('dp', None, 'fsdp'), as said below
- left_stats: float32 [96, 32, 4, 8, 1024], P('fsdp', None, 'dp'), as said below
- right_stats: float32 [96, 32, 4, 8, 1024], P('fsdp', None, 'dp'), as said below
- accum: float32 [96, 32, 4, 8, 1024], P('fsdp', None, 'dp'), may hold values from 0.001 to 0.1
- left_root: bfloat16 [96, 32, 4, 8, 1024], P('fsdp', None, 'dp'), as said below
- right_root: bfloat16 [96, 32, 4, 8, 1024], P('fsdp', None, 'dp'), as said below
- owner_slot: int32 [36], replicated, may hold values from 0 to 95, as said below
Outputs:
- update: bfloat16 [36, 1024, 1024], P(None, 'fsdp')
- left_new: float32 [96, 32, 4, 8, 1024], P('fsdp', None, 'dp')
- right_new: float32 [96, 32, 4, 8, 1024], P('fsdp', None, 'dp')
- accum_new: float32 [96, 32, 4, 8, 1024], P('fsdp', None, 'dp')
Inputs may be any that keep to these rules, and one draw needn't show every extreme that they name: Entries are distinct; block b lives on owner owner_slot[b] // 3 in its slot owner_slot[b] % 3; in every draw some owner has all 3 slots in use, which one drawn from the seed. `grad_parts`: each block's rows and columns carry their own scales. `left_stats`: positive diagonal with independent off-diagonal entries. `right_stats`: positive diagonal with independent off-diagonal entries. `left_root`: positive diagonal with independent off-diagonal entries. `right_root`: positive diagonal with independent off-diagonal entries.
All inputs are finite; a program needn't handle non-finite values.
Results may differ from a plain program's by a relative error of at most 0.023.
Values may be sent and summed in bfloat16 or wider, within the bound.
A program may use at most 192 MiB of HBM per device.

v0:
```python
import functools

import jax
import jax.numpy as jnp
from jax import lax
from jax.experimental import pallas as pl
from jax.experimental.pallas import tpu as pltpu
from jax.sharding import PartitionSpec as P

MESH = pl.DeviceIdType.MESH
BF = jnp.bfloat16
F32 = jnp.float32
STEP = 13
STEP_VMEM = 60 << 20
FINISH_VMEM = 60 << 20


def dot(a, b):
    return jnp.dot(a, b, preferred_element_type=F32)


def dot_t(a, b):
    return lax.dot_general(a, b, (((1,), (1,)), ((), ())), preferred_element_type=F32)


def step_kernel(
    N, S, F, W,
    own_ref, gp, lr, rr, ac,
    sl_out, sr_out, gm_out, up_out, tab_out,
    ra, rb, fa_raw, fb_raw, ca, cb, fa_comb, fb_comb,
    red_own, red_l, red_r, red_o,
    sb, gb, rraw, rn, rv, lv, av, sel, hf, pv, gct, gmb, ls, rs_,
    pb, u_0, u_1, u_2, uall, nb, tab_v, tab,
    rs_s, rs_r, ag_s, ag_r, rt_s, rt_r, g_s, g_r, p_s, p_r, n_s, n_r, u_s, u_r, loc, outs,
):
    H = N // 2
    W2 = W // 2
    B = F * 32
    SH = F * 8
    T = 256 if W % 256 == 0 else W
    NT = W // T
    nx = 4 if F >= 32 else 2
    nz = F // (2 * nx)
    d = lax.axis_index("dp")
    f = lax.axis_index("fsdp")
    z = f // (2 * nx)
    x = (f // 2) % nx
    c = f % 2
    e1, e2, e3 = lax.rem(d + 1, 4), lax.rem(d + 2, 4), lax.rem(d + 3, 4)
    right, left, opp = (e1, f), (e3, f), (e2, f)
    lo, hi = pl.ds(0, H), pl.ds(H, H)

    def peer(i):
        o = lax.rem(i * STEP, F)
        pz = lax.rem(z + o // (2 * nx), nz)
        px = lax.rem(x + (o // 2) % nx, nx)
        pc = lax.rem(c + o % 2, 2)
        return (pz * nx + px) * 2 + pc

    def rcopy(src, dst, ss, rs, dev):
        return pltpu.make_async_remote_copy(
            src_ref=src, dst_ref=dst, send_sem=ss, recv_sem=rs, device_id=dev, device_id_type=MESH
        )

    def rows(e):
        return pl.ds(pl.multiple_of((e // 2) * 16, 16), 16)

    def cols(e):
        return pl.ds(pl.multiple_of((e % 2) * W2, W2), W2)

    def within(v, top):
        return jnp.minimum(jnp.maximum(v, 0), top)

    def loop(n, fn, unroll=1):
        lax.fori_loop(0, n, lambda i, _: (fn(i), 0)[1], 0, unroll=unroll)

    ld_l = pltpu.make_async_copy(lr, lv, loc.at[0])
    ld_l.start()
    ld_a = pltpu.make_async_copy(ac, av, loc.at[1])
    ld_a.start()
    ld_r = pltpu.make_async_copy(rr, rv, loc.at[2])
    ld_r.start()

    barrier = pltpu.get_barrier_semaphore()

    def greet(i):
        pl.semaphore_signal(barrier, inc=1, device_id=(d, peer(i + 1)), device_id_type=MESH)

    for dev in (right, left, opp):
        pl.semaphore_signal(barrier, inc=1, device_id=dev, device_id_type=MESH)
    loop(F - 1, greet)
    for ref in (red_own, red_l, red_r, red_o):
        ref[N] = jnp.zeros((16, W2), BF)
    us = (u_0, u_1, u_2)
    for ref in us:
        ref[F] = jnp.zeros((16, W2), BF)
    pick = lax.broadcasted_iota(jnp.int32, (SH, B), 0)
    at = lax.broadcasted_iota(jnp.int32, (SH, B), 1)
    sel[...] = jnp.where(at == (pick // 8) * 32 + d * 8 + pick % 8, 1.0, 0.0).astype(BF)
    pl.semaphore_wait(barrier, F + 2)

    def tables():
        lanes = 128

        def iota(shape, dim):
            return lax.broadcasted_iota(jnp.int32, shape, dim).astype(F32)

        def count(cond, axis):
            return jnp.sum(jnp.where(cond, 1.0, 0.0), axis=axis, keepdims=True)

        down, along = iota((N, N), 0), iota((N, N), 1)
        own_r = own_ref[...].astype(F32)
        own_rr = jnp.broadcast_to(own_r, (N, N))
        own_c = jnp.sum(jnp.where(down == along, own_rr, 0.0), axis=1, keepdims=True)
        own_cc = jnp.broadcast_to(own_c, (N, N))
        q_r = jnp.floor((own_r + 0.5) * (1.0 / S))
        q_c = jnp.floor((own_c + 0.5) * (1.0 / S))
        same = jnp.broadcast_to(q_c, (N, N)) == jnp.broadcast_to(q_r, (N, N))
        rank_r = count(same & (own_cc < own_rr), 0)
        rank_c = count(same & (own_rr < own_cc), 1)
        rk_r = jnp.broadcast_to(rank_r, (N, N))
        rk_c = jnp.broadcast_to(rank_c, (N, N))
        pos_r = count((rk_c < rk_r) | ((rk_c == rk_r) & (down < along)), 0)
        pos_c = count((rk_r < rk_c) | ((rk_r == rk_c) & (along < down)), 1)
        lane = iota((N, lanes), 1)
        block = iota((N, lanes), 0)
        lane_q = jnp.floor((lane + 0.5) * (1.0 / S))
        lane_r = lane - S * lane_q
        qw = jnp.broadcast_to(q_c, (N, lanes))
        rw = jnp.broadcast_to(rank_c, (N, lanes))
        ow = jnp.broadcast_to(own_c, (N, lanes))
        pw = jnp.broadcast_to(pos_c, (N, lanes))
        inv = jnp.min(
            jnp.where((qw == lane_q) & (rw == lane_r), block, float(N)), axis=0, keepdims=True
        )
        ord_q = jnp.sum(jnp.where(pw == lane, qw, 0.0), axis=0, keepdims=True)
        ord_r = jnp.sum(jnp.where(pw == lane, rw, 0.0), axis=0, keepdims=True)
        base = (f * S).astype(F32)
        here = qw == f.astype(F32)
        total = count(here, 0)
        low = count(here & (ow < base + lane), 0)
        used = count(ow == base + lane, 0)
        rank_s = jnp.where(used > 0.5, low, total + lane[0:1] - low)
        tab_v[0:1, :] = inv.astype(jnp.int32)
        tab_v[1:2, :] = ord_q.astype(jnp.int32)
        tab_v[2:3, :] = ord_r.astype(jnp.int32)
        tab_v[3:4, :] = rank_s.astype(jnp.int32)
        tab_v[4:5, :] = jnp.zeros((1, lanes), jnp.int32)
        tab_v[4:5, 0:N] = pos_r.astype(jnp.int32)
        tab_v[5:8, :] = jnp.zeros((3, lanes), jnp.int32)

    c1 = rcopy(gp.at[lo, rows(e2), cols(e2)], ra, rs_s.at[0], rs_r.at[0], right)
    c2 = rcopy(gp.at[hi, rows(e2), cols(e2)], rb, rs_s.at[1], rs_r.at[1], left)
    c3 = rcopy(gp.at[hi, rows(e1), cols(e1)], fb_raw, rs_s.at[2], rs_r.at[2], right)
    c4 = rcopy(gp.at[lo, rows(e3), cols(e3)], fa_raw, rs_s.at[3], rs_r.at[3], left)
    c5 = rcopy(ca, fa_comb, rs_s.at[4], rs_r.at[4], right)
    c6 = rcopy(cb, fb_comb, rs_s.at[5], rs_r.at[5], left)
    c1.start()
    c2.start()
    c3.start()
    c4.start()
    tables()
    to_scalars = pltpu.make_async_copy(tab_v, tab, loc.at[3 + S])
    to_scalars.start()
    to_scalars.wait()
    perm = []
    for r in range(S):
        k = jnp.int32(0)
        for s in range(1, S):
            k = jnp.where(tab[3, s] == r, s, k)
        perm.append(within(k, S - 1))
    ld_r.wait()

    def reorder(t):
        part = pl.ds(pl.multiple_of(t * 16, 16), 16)
        for r in range(S):
            rraw[d, r, part, :] = rv[perm[r], part, :]

    loop(SH // 16, reorder)
    c1.wait_recv()

    def add_a(b):
        ca[b] = (ra[b].astype(F32) + gp[b, rows(e1), cols(e1)].astype(F32)).astype(BF)

    loop(H, add_a)
    c5.start()
    c2.wait_recv()

    def add_b(b):
        cb[b] = (rb[b].astype(F32) + gp[H + b, rows(e3), cols(e3)].astype(F32)).astype(BF)

    loop(H, add_b)
    c6.start()
    c4.wait_recv()
    c5.wait_recv()

    def fin_a(b):
        own = gp[b, rows(d), cols(d)].astype(F32)
        red_own[b] = (own + fa_raw[b].astype(F32) + fa_comb[b].astype(F32)).astype(BF)

    loop(H, fin_a)
    c3.wait_recv()
    c6.wait_recv()

    def fin_b(b):
        own = gp[H + b, rows(d), cols(d)].astype(F32)
        red_own[H + b] = (own + fb_raw[b].astype(F32) + fb_comb[b].astype(F32)).astype(BF)

    loop(H, fin_b)

    every = pl.ds(0, N)
    a1 = rcopy(red_own.at[every], red_l.at[every], ag_s.at[0], ag_r.at[0], right)
    a2 = rcopy(red_own.at[every], red_r.at[every], ag_s.at[1], ag_r.at[1], left)
    a3 = rcopy(red_l.at[lo], red_o.at[lo], ag_s.at[2], ag_r.at[2], right)
    a4 = rcopy(red_r.at[hi], red_o.at[hi], ag_s.at[3], ag_r.at[3], left)
    a1.start()
    a2.start()

    HR = SH // 2
    up_, dn_ = pl.ds(0, HR), pl.ds(HR, HR)

    def root(s):
        return (
            rcopy(rraw.at[d, s], rraw.at[d, s], rt_s.at[s, 0], rt_r.at[s, 0], right),
            rcopy(rraw.at[d, s], rraw.at[d, s], rt_s.at[s, 1], rt_r.at[s, 1], left),
            rcopy(rraw.at[e3, s, up_], rraw.at[e3, s, up_], rt_s.at[s, 2], rt_r.at[s, 2], right),
            rcopy(rraw.at[e1, s, dn_], rraw.at[e1, s, dn_], rt_s.at[s, 3], rt_r.at[s, 3], left),
        )

    roots = [root(s) for s in range(S)]

    def start_root(s):
        roots[s][0].start()
        roots[s][1].start()

    def forward_root(s):
        roots[s][0].wait_recv()
        roots[s][2].start()
        roots[s][1].wait_recv()
        roots[s][3].start()

    def place(red, e):
        def one(q):
            for s in range(S):
                sb[s, q, rows(e), cols(e)] = red[within(tab[0, q * S + s], N)]

        loop(F, one)

    def send_quarter(s, e):
        def one(i):
            q = peer(i + 1)
            rcopy(
                sb.at[s, q, rows(e), cols(e)],
                gb.at[s, f, rows(e), cols(e)],
                g_s.at[s], g_r.at[s], (d, q),
            ).start()

        loop(F - 1, one)

    def send_whole(s):
        def one(i):
            q = peer(i + 1)
            rcopy(sb.at[s, q], gb.at[s, f], g_s.at[s], g_r.at[s], (d, q)).start()

        loop(F - 1, one)

    place(red_own, d)
    send_quarter(0, d)
    a1.wait_recv()
    a3.start()
    a2.wait_recv()
    a4.start()
    start_root(0)
    place(red_l, e3)
    send_quarter(0, e3)
    place(red_r, e1)
    send_quarter(0, e1)
    a3.wait_recv()
    a4.wait_recv()
    place(red_o, e2)
    send_quarter(0, e2)
    selfs = [pltpu.make_async_copy(sb.at[s, f], gb.at[s, f], loc.at[3 + s]) for s in range(S)]
    for s in range(S):
        selfs[s].start()
    for s in range(1, S):
        send_whole(s)
    forward_root(0)
    if S > 1:
        start_root(1)
    ld_l.wait()
    ld_a.wait()

    def tile(j):
        return pl.ds(pl.multiple_of(j * T, T), T)

    def gcols(s, j):
        return gb[s, :, :, tile(j)].reshape(B, T)

    def grows(s, j):
        return gb[s, pl.ds(j * (T // 32), T // 32)].reshape(T, W)

    out_copies = []

    def put(src, dst, k):
        cp = pltpu.make_async_copy(src, dst, outs.at[k])
        cp.start()
        out_copies.append(cp)

    def others(n):
        return pl.ds(0, n)

    def third(t):
        n = N // S
        own = pl.ds(t * n, n)
        a, b = pl.ds(t * n, n // 2), pl.ds(t * n + n // 2, n - n // 2)
        return (
            rcopy(uall.at[d, own], uall.at[d, own], u_s.at[t, 0], u_r.at[t, 0], right),
            rcopy(uall.at[d, own], uall.at[d, own], u_s.at[t, 1], u_r.at[t, 1], left),
            rcopy(uall.at[e3, a], uall.at[e3, a], u_s.at[t, 2], u_r.at[t, 2], right),
            rcopy(uall.at[e1, b], uall.at[e1, b], u_s.at[t, 3], u_r.at[t, 3], left),
        )

    up_copies = [third(t) for t in range(S)]

    def start_third(t):
        rcopy(
            pb.at[t, others(F - 1)], us[t].at[others(F - 1)], p_s.at[t], p_r.at[t], right
        ).wait_recv()

        def choose(i):
            j = t * (N // S) + i
            q, r = within(tab[1, j], F), tab[2, j]
            v = us[0][jnp.where(r == 0, q, F)].astype(F32)
            for k in range(1, t + 1):
                v = v + us[k][jnp.where(r == k, q, F)].astype(F32)
            uall[d, j] = v.astype(BF)

        loop(N // S, choose)
        up_copies[t][0].start()
        up_copies[t][1].start()

    def forward_third(t):
        up_copies[t][0].wait_recv()
        up_copies[t][2].start()
        up_copies[t][1].wait_recv()
        up_copies[t][3].start()

    def statistics(s):
        def left_stat(j):
            g = grows(s, j)
            ls[s, :, tile(j)] = dot_t(gmb[s], g).astype(BF)
            gct[:, tile(j)] = dot_t(sel[...], g).astype(BF)

        loop(NT, left_stat)

        def right_stat(j):
            rs_[s, :, tile(j)] = dot(gct[...], gcols(s, j)).astype(BF)

        loop(NT, right_stat)
        put(gmb.at[s], gm_out.at[s], 3 * s)
        put(ls.at[s], sl_out.at[s], 3 * s + 1)
        put(rs_.at[s], sr_out.at[s], 3 * s + 2)

    for s in range(S):
        rcopy(sb.at[s, others(F - 1)], gb.at[s, others(F - 1)], g_s.at[s], g_r.at[s], right).wait_recv()
        selfs[s].wait()

        def halves(j):
            hf[:, tile(j)] = dot(lv[perm[s]], gcols(s, j)).astype(BF)

        loop(NT, halves)

        def mine(j, dn):
            g = dot(sel[...], gcols(s, j))
            gmb[s, :, tile(j)] = g.astype(BF)
            an = av[perm[s], :, tile(j)] + g * g
            dr = g * lax.rsqrt(an)
            return dn + jnp.sum(dr * dr)

        dn = lax.fori_loop(0, NT, mine, jnp.float32(0))

        roots[s][2].wait_recv()
        roots[s][3].wait_recv()

        def weave(t):
            part = [rraw[e, s, pl.ds(pl.multiple_of(t * 16, 16), 16), :].astype(F32) for e in range(4)]
            for h in range(2):
                rows32 = jnp.concatenate([p[8 * h : 8 * h + 8] for p in part], axis=0)
                rn[pl.ds(pl.multiple_of(t * 64 + 32 * h, 32), 32), :] = rows32.astype(BF)

        loop(F // 2, weave)

        def prec(j, pn):
            p = dot(hf[...], rn[:, tile(j)])
            pv[:, tile(j)] = p
            return pn + jnp.sum(p * p)

        pn = lax.fori_loop(0, NT, prec, jnp.float32(0))

        nb[s, d, 0] = jnp.full((8, 128), dn, F32)
        nb[s, d, 1] = jnp.full((8, 128), pn, F32)
        ns = [
            rcopy(nb.at[s, d], nb.at[s, d], n_s.at[s, k], n_r.at[s, k], dev)
            for k, dev in enumerate((right, left, opp))
        ]
        for cp in ns:
            cp.start()
        if s + 1 < S:
            forward_root(s + 1)
            if s + 2 < S:
                start_root(s + 2)
        for cp in ns:
            cp.wait()
        dsum = nb[s, 0, 0] + nb[s, 1, 0] + nb[s, 2, 0] + nb[s, 3, 0]
        psum = nb[s, 0, 1] + nb[s, 1, 1] + nb[s, 2, 1] + nb[s, 3, 1]
        factor = jnp.sqrt(dsum / (psum + 1e-06))[0:1, 0:1]

        def scale(q):
            v = pv[pl.ds(pl.multiple_of(q * 8, 8), 8), :] * factor
            pb[s, q] = jnp.concatenate([v[:, :W2], v[:, W2:]], axis=0).astype(BF)

        loop(F, scale)
        us[s][f] = pb[s, f]

        def send_p(i):
            q = peer(i + 1)
            rcopy(pb.at[s, q], us[s].at[f], p_s.at[s], p_r.at[s], (d, q)).start()

        loop(F - 1, send_p)
        if s >= 1:
            start_third(s - 1)
        statistics(s)
        if s >= 1:
            forward_third(s - 1)

    start_third(S - 1)
    forward_third(S - 1)
    for t in range(S):
        up_copies[t][2].wait_recv()
        up_copies[t][3].wait_recv()
    put(uall, up_out, 3 * S)
    put(tab_v, tab_out, 3 * S + 1)

    for cp in (c1, c2, c3, c4, c5, c6, a1, a2, a3, a4):
        cp.wait_send()
    for s in range(S):
        for cp in up_copies[s]:
            cp.wait_send()
        for cp in roots[s]:
            cp.wait_send()
        rcopy(sb.at[s, others(F - 1)], gb.at[s, others(F - 1)], g_s.at[s], g_r.at[s], right).wait_send()
        rcopy(pb.at[s, others(F - 1)], us[s].at[others(F - 1)], p_s.at[s], p_r.at[s], right).wait_send()
    for cp in out_copies:
        cp.wait()


def finish_kernel(nb, tab, *refs):
    ups, (sl, sr, gm, left, right, acc, up_o, left_o, right_o, acc_o) = refs[:nb], refs[nb:]
    for b in range(nb):
        parts = []
        for e in range(4):
            v = ups[b][e, 0].astype(F32)
            parts.append(jnp.concatenate([v[:8], v[8:]], axis=1))
        up_o[b] = jnp.concatenate(parts, axis=0).astype(BF)
    left_o[...] = 0.95 * left[...] + 0.05 * sl[...].astype(F32)
    right_o[...] = 0.95 * right[...] + 0.05 * sr[...].astype(F32)
    g = gm[...].astype(F32)
    acc_o[...] = acc[...] + g * g


def body(grad_parts, left_stats, right_stats, accum, left_root, right_root, owner_slot):
    N = owner_slot.shape[0]
    F = lax.axis_size("fsdp")
    S = left_stats.shape[0]
    W = left_stats.shape[4]
    SH = F * 8
    H = N // 2
    W2 = W // 2
    hbm = pl.BlockSpec(memory_space=pl.ANY)
    vmem = pl.BlockSpec(memory_space=pltpu.VMEM)
    half = pltpu.VMEM((H, 16, W2), BF)
    whole = pltpu.VMEM((N + 1, 16, W2), BF)
    dma = pltpu.SemaphoreType.DMA
    share = jax.ShapeDtypeStruct((S, SH, W), BF)
    sl, sr, gm, up, tab = pl.pallas_call(
        functools.partial(step_kernel, N, S, F, W),
        out_shape=(share, share, share, jax.ShapeDtypeStruct((4, N, 16, W2), BF),
                   jax.ShapeDtypeStruct((8, 128), jnp.int32)),
        in_specs=[vmem, vmem, hbm, hbm, hbm],
        out_specs=(hbm,) * 5,
        scratch_shapes=[half] * 8
        + [whole] * 4
        + [
            pltpu.VMEM((S, F, 32, W), BF),
            pltpu.VMEM((S, F, 32, W), BF),
            pltpu.VMEM((4, S, SH, W), BF),
            pltpu.VMEM((F * 32, W), BF),
            pltpu.VMEM((S, SH, W), BF),
            pltpu.VMEM((S, SH, W), BF),
            pltpu.VMEM((S, SH, W), F32),
            pltpu.VMEM((SH, F * 32), BF),
            pltpu.VMEM((SH, W), BF),
            pltpu.VMEM((SH, W), F32),
            pltpu.VMEM((SH, F * 32), BF),
            pltpu.VMEM((S, SH, W), BF),
            pltpu.VMEM((S, SH, W), BF),
            pltpu.VMEM((S, SH, W), BF),
            pltpu.VMEM((S, F, 16, W2), BF),
            pltpu.VMEM((F + 1, 16, W2), BF),
            pltpu.VMEM((F + 1, 16, W2), BF),
            pltpu.VMEM((F + 1, 16, W2), BF),
            pltpu.VMEM((4, N, 16, W2), BF),
            pltpu.VMEM((S, 4, 2, 8, 128), F32),
            pltpu.VMEM((8, 128), jnp.int32),
            pltpu.SMEM((8, 128), jnp.int32),
        ]
        + [
            dma((6,)), dma((6,)), dma((4,)), dma((4,)), dma((S, 4)), dma((S, 4)),
            dma((S,)), dma((S,)), dma((S,)), dma((S,)), dma((S, 3)), dma((S, 3)),
            dma((S, 4)), dma((S, 4)), dma((4 + S,)), dma((3 * S + 2,)),
        ],
        compiler_params=pltpu.CompilerParams(
            collective_id=0, has_side_effects=True, vmem_limit_bytes=STEP_VMEM
        ),
        name="shampoo_step",
    )(
        owner_slot[None, :], grad_parts[0],
        left_root.reshape(S, SH, W), right_root.reshape(S, SH, W), accum.reshape(S, SH, W),
    )
    rows = S * SH
    K = 12 if N % 12 == 0 and rows % 12 == 0 and (rows // 12) % 16 == 0 else S
    nb, rb = N // K, rows // K
    per = K // S
    flat = pl.BlockSpec((rb, W), lambda i, tab: (i, 0))
    ranked = pl.BlockSpec((rb, W), lambda i, tab: (tab[3, i // per] * per + i % per, 0))
    picked = [
        pl.BlockSpec((4, 1, 16, W2), lambda i, tab, k=k: (0, tab[4, i * nb + k], 0, 0))
        for k in range(nb)
    ]
    stat = jax.ShapeDtypeStruct((rows, W), F32)
    update, left_out, right_out, accu_out = pl.pallas_call(
        functools.partial(finish_kernel, nb),
        grid_spec=pltpu.PrefetchScalarGridSpec(
            num_scalar_prefetch=1,
            grid=(K,),
            in_specs=picked + [ranked] * 3 + [flat] * 3,
            out_specs=(pl.BlockSpec((nb, 32, W), lambda i, tab: (i, 0, 0)), flat, flat, flat),
        ),
        out_shape=(jax.ShapeDtypeStruct((N, 32, W), BF), stat, stat, stat),
        compiler_params=pltpu.CompilerParams(vmem_limit_bytes=FINISH_VMEM),
        name="shampoo_finish",
    )(
        tab, *([up] * nb), sl.reshape(rows, W), sr.reshape(rows, W), gm.reshape(rows, W),
        left_stats.reshape(rows, W), right_stats.reshape(rows, W), accum.reshape(rows, W),
    )
    layout = left_stats.shape
    return (update, left_out.reshape(layout), right_out.reshape(layout), accu_out.reshape(layout))


def solution(mesh):
    spread = P("fsdp", None, "dp", None, None)
    return jax.shard_map(
        body,
        mesh=mesh,
        in_specs=(P("dp", None, "fsdp", None),) + (spread,) * 5 + (P(),),
        out_specs=(P(None, "fsdp", None), spread, spread, spread),
        check_vma=False,
    )
```

profile of v0, /device:TPU:1, one launch (start us, length us, event | category | flops | bytes accessed | tf_op | source)
XLA Modules:
  0.0 174.1 jit_solution(15508930402485315447)
XLA Ops:
  0.6 159.1 %shampoo_step.1 = (bf16[3,256,1024]{2,1,0:T(8,128)(2,1)}, bf16[3,256,1024]{2,1,0:T(8,128)(2,1)}, bf16[3,256,1024]{2,1,0:T(8,128)(2,1)}, bf16[4,36,16,512]{3,2,1,0:T(8,128)(2,1)}, s32[8,128]{1,0:T(8,128)}) custom-call(s32[1,36]{1,0:T(1,128)} %bitcast.30, bf16[36,32,1024]{2,1,0:T(8,128)(2,1)} %bitcast.24, bf16[3,256,1024]{2,1,0:T(8,128)(2,1)} %bitcast.28, ...), custom_call_target="tpu_custom_call" | custom-call | tf_op jit(solution)/shard_map/shampoo_step/pallas_call | solution.py:485
  159.7 14.4 %shampoo_finish.1 = (bf16[36,32,1024]{2,1,0:T(8,128)(2,1)}, f32[768,1024]{1,0:T(8,128)}, f32[768,1024]{1,0:T(8,128)}, f32[768,1024]{1,0:T(8,128)}) custom-call(s32[8,128]{1,0:T(8,128)} %get-tuple-element.13.tab, bf16[4,36,16,512]{3,2,1,0:T(8,128)(2,1)} %get-tuple-element.14.refs_0_.refs_1_.refs_2_, ...), custom_call_target="tpu_custom_call" | custom-call | tf_op jit(solution)/shard_map/shampoo_finish/pallas_call | solution.py:541
where the time goes:
time: 175 us; the launch traced here: 174 us
  Pallas kernels  173 us (99%)
    pallas_call x1, Pallas kernels, body(): pl.pallas_call(functools.partial(step_kernel, N, S, F, W), out_shape=(sha...  159 us
    pallas_call x1, Pallas kernels, body(): pl.pallas_call(functools.partial(finish_kernel, nb), grid_spec=pltpu.Pref...  14.4 us

commit v1 on v0

v1 whole, which is shorter than its diff:
```python
import functools

import jax
import jax.numpy as jnp
from jax import lax
from jax.experimental import pallas as pl
from jax.experimental.pallas import tpu as pltpu
from jax.sharding import PartitionSpec as P

MESH = pl.DeviceIdType.MESH
BF = jnp.bfloat16
F32 = jnp.float32
STEP = 5
STEP_VMEM = 45 << 20
FINISH_VMEM = 18 << 20


def dot(a, b):
    return jnp.dot(a, b, preferred_element_type=F32)


def dot_t(a, b):
    return lax.dot_general(a, b, (((1,), (1,)), ((), ())), preferred_element_type=F32)


def step_kernel(
    N, S, F, W,
    own_ref, gp_in, lr, rr, ac,
    sl_out, sr_out, an_0, an_1, an_2, up_0, up_1, up_2, up_3, nm_out, tab_out,
    gp, ra, rb, fa_raw, fb_raw, ca, cb, fa_comb, fb_comb,
    red_own_0, red_own_1, red_l_0, red_l_1, red_r_0, red_r_1, red_o_0, red_o_1,
    sb, gb, rraw, rn, rv, lv, av, sel, hf, pv, gct, gmb, anb, ls, rs_,
    pb, u_0, u_1, u_2, uall, nb, nl_0, nl_1, nl_2, nall, tab_v, tab,
    rs_s, rs_r, ag_s, ag_r, rt_s, rt_r, g_s, g_r, p_s, p_r, w_s, w_r, n_s, n_r, u_s, u_r, loc, outs,
):
    H = N // 2
    W2, W4 = W // 2, W // 4
    B = F * 32
    SH = F * 8
    T = 256 if W % 256 == 0 else W
    NT = W // T
    nx = 4 if F >= 32 else 2
    nz = F // (2 * nx)
    d = lax.axis_index("dp")
    f = lax.axis_index("fsdp")
    z = f // (2 * nx)
    x = (f // 2) % nx
    c = f % 2
    e1, e2, e3 = lax.rem(d + 1, 4), lax.rem(d + 2, 4), lax.rem(d + 3, 4)
    right, left, opp = (e1, f), (e3, f), (e2, f)
    lo, hi = pl.ds(0, H), pl.ds(H, H)

    def peer(i):
        o = lax.rem(i * STEP, F)
        pz = lax.rem(z + o // (2 * nx), nz)
        px = lax.rem(x + (o // 2) % nx, nx)
        pc = lax.rem(c + o % 2, 2)
        return (pz * nx + px) * 2 + pc

    def rcopy(src, dst, ss, rs, dev):
        return pltpu.make_async_remote_copy(
            src_ref=src, dst_ref=dst, send_sem=ss, recv_sem=rs, device_id=dev, device_id_type=MESH
        )

    def rows(e):
        return pl.ds(pl.multiple_of((e // 2) * 16, 16), 16)

    def cols(e):
        return pl.ds(pl.multiple_of((e % 2) * W2, W2), W2)

    def within(v, top):
        return jnp.minimum(jnp.maximum(v, 0), top)

    def cols4(e, h):
        return pl.ds(pl.multiple_of((e % 2) * W2 + h * W4, W4), W4)

    def part(h):
        return pl.ds(h * W4, W4)

    def loop(n, fn, unroll=1):
        lax.fori_loop(0, n, lambda i, _: (fn(i), 0)[1], 0, unroll=unroll)

    ld_g = pltpu.make_async_copy(gp_in, gp, loc.at[4 + S])
    ld_g.start()
    ld_l = pltpu.make_async_copy(lr, lv, loc.at[0])
    ld_l.start()
    ld_a = pltpu.make_async_copy(ac, av, loc.at[1])
    ld_a.start()
    ld_r = pltpu.make_async_copy(rr, rv, loc.at[2])
    ld_r.start()

    barrier = pltpu.get_barrier_semaphore()

    def greet(i):
        pl.semaphore_signal(barrier, inc=1, device_id=(d, peer(i + 1)), device_id_type=MESH)

    for dev in (right, left, opp):
        pl.semaphore_signal(barrier, inc=1, device_id=dev, device_id_type=MESH)
    loop(F - 1, greet)
    red_own, red_l = (red_own_0, red_own_1), (red_l_0, red_l_1)
    red_r, red_o = (red_r_0, red_r_1), (red_o_0, red_o_1)
    for ref in red_own + red_l + red_r + red_o:
        ref[N] = jnp.zeros((16, W4), BF)
    us = (u_0, u_1, u_2)
    for ref in us:
        ref[F] = jnp.zeros((16, W2), BF)
    nls = (nl_0, nl_1, nl_2)
    for ref in nls:
        ref[F] = jnp.zeros((1, 128), F32)
    pick = lax.broadcasted_iota(jnp.int32, (SH, B), 0)
    at = lax.broadcasted_iota(jnp.int32, (SH, B), 1)
    sel[...] = jnp.where(at == (pick // 8) * 32 + d * 8 + pick % 8, 1.0, 0.0).astype(BF)
    pl.semaphore_wait(barrier, F + 2)

    def tables():
        lanes = 128

        def iota(shape, dim):
            return lax.broadcasted_iota(jnp.int32, shape, dim).astype(F32)

        def count(cond, axis):
            return jnp.sum(jnp.where(cond, 1.0, 0.0), axis=axis, keepdims=True)

        down, along = iota((N, N), 0), iota((N, N), 1)
        own_r = own_ref[...].astype(F32)
        own_rr = jnp.broadcast_to(own_r, (N, N))
        own_c = jnp.sum(jnp.where(down == along, own_rr, 0.0), axis=1, keepdims=True)
        own_cc = jnp.broadcast_to(own_c, (N, N))
        q_r = jnp.floor((own_r + 0.5) * (1.0 / S))
        q_c = jnp.floor((own_c + 0.5) * (1.0 / S))
        same = jnp.broadcast_to(q_c, (N, N)) == jnp.broadcast_to(q_r, (N, N))
        rank_r = count(same & (own_cc < own_rr), 0)
        rank_c = count(same & (own_rr < own_cc), 1)
        rk_r = jnp.broadcast_to(rank_r, (N, N))
        rk_c = jnp.broadcast_to(rank_c, (N, N))
        pos_r = count((rk_c < rk_r) | ((rk_c == rk_r) & (down < along)), 0)
        pos_c = count((rk_r < rk_c) | ((rk_r == rk_c) & (along < down)), 1)
        lane = iota((N, lanes), 1)
        block = iota((N, lanes), 0)
        lane_q = jnp.floor((lane + 0.5) * (1.0 / S))
        lane_r = lane - S * lane_q
        qw = jnp.broadcast_to(q_c, (N, lanes))
        rw = jnp.broadcast_to(rank_c, (N, lanes))
        ow = jnp.broadcast_to(own_c, (N, lanes))
        pw = jnp.broadcast_to(pos_c, (N, lanes))
        inv = jnp.min(
            jnp.where((qw == lane_q) & (rw == lane_r), block, float(N)), axis=0, keepdims=True
        )
        ord_q = jnp.sum(jnp.where(pw == lane, qw, 0.0), axis=0, keepdims=True)
        ord_r = jnp.sum(jnp.where(pw == lane, rw, 0.0), axis=0, keepdims=True)
        base = (f * S).astype(F32)
        here = qw == f.astype(F32)
        total = count(here, 0)
        low = count(here & (ow < base + lane), 0)
        used = count(ow == base + lane, 0)
        rank_s = jnp.where(used > 0.5, low, total + lane[0:1] - low)
        tab_v[0:1, :] = inv.astype(jnp.int32)
        tab_v[1:2, :] = ord_q.astype(jnp.int32)
        tab_v[2:3, :] = ord_r.astype(jnp.int32)
        tab_v[3:4, :] = rank_s.astype(jnp.int32)
        tab_v[4:5, :] = jnp.zeros((1, lanes), jnp.int32)
        tab_v[4:5, 0:N] = pos_r.astype(jnp.int32)
        tab_v[5:8, :] = jnp.zeros((3, lanes), jnp.int32)

    def sums(h):
        p, ss, rs = part(h), rs_s, rs_r
        every_a = (slice(None), slice(None), p)
        return (
            rcopy(gp_in.at[lo, rows(e2), cols4(e2, h)], ra.at[every_a], ss.at[h, 0], rs.at[h, 0], right),
            rcopy(gp_in.at[hi, rows(e2), cols4(e2, h)], rb.at[every_a], ss.at[h, 1], rs.at[h, 1], left),
            rcopy(gp_in.at[hi, rows(e1), cols4(e1, h)], fb_raw.at[every_a], ss.at[h, 2], rs.at[h, 2], right),
            rcopy(gp_in.at[lo, rows(e3), cols4(e3, h)], fa_raw.at[every_a], ss.at[h, 3], rs.at[h, 3], left),
            rcopy(ca.at[every_a], fa_comb.at[every_a], ss.at[h, 4], rs.at[h, 4], right),
            rcopy(cb.at[every_a], fb_comb.at[every_a], ss.at[h, 5], rs.at[h, 5], left),
        )

    def relay(h):
        c, p = halves_of_sum[h], part(h)
        c[0].wait_recv()

        def add_a(b):
            ca[b, :, p] = (ra[b, :, p].astype(F32) + gp[b, rows(e1), cols4(e1, h)].astype(F32)).astype(BF)

        loop(H, add_a)
        c[4].start()
        c[1].wait_recv()

        def add_b(b):
            cb[b, :, p] = (
                rb[b, :, p].astype(F32) + gp[H + b, rows(e3), cols4(e3, h)].astype(F32)
            ).astype(BF)

        loop(H, add_b)
        c[5].start()

    def total(h):
        c, p = halves_of_sum[h], part(h)
        c[3].wait_recv()
        c[4].wait_recv()

        def fin_a(b):
            own = gp[b, rows(d), cols4(d, h)].astype(F32)
            red_own[h][b] = (
                own + fa_raw[b, :, p].astype(F32) + fa_comb[b, :, p].astype(F32)
            ).astype(BF)

        loop(H, fin_a)
        c[2].wait_recv()
        c[5].wait_recv()

        def fin_b(b):
            own = gp[H + b, rows(d), cols4(d, h)].astype(F32)
            red_own[h][H + b] = (
                own + fb_raw[b, :, p].astype(F32) + fb_comb[b, :, p].astype(F32)
            ).astype(BF)

        loop(H, fin_b)

    halves_of_sum = [sums(h) for h in range(2)]
    for k in range(4):
        halves_of_sum[0][k].start()
    tables()
    to_scalars = pltpu.make_async_copy(tab_v, tab, loc.at[3])
    to_scalars.start()
    to_scalars.wait()
    perm = []
    for r in range(S):
        k = jnp.int32(0)
        for s in range(1, S):
            k = jnp.where(tab[3, s] == r, s, k)
        perm.append(within(k, S - 1))
    ld_r.wait()

    def reorder(t):
        part = pl.ds(pl.multiple_of(t * 16, 16), 16)
        for r in range(S):
            rraw[d, r, part, :] = rv[perm[r], part, :]

    loop(SH // 16, reorder)

    every = pl.ds(0, N)

    def gathers(h):
        return (
            rcopy(red_own[h].at[every], red_l[h].at[every], ag_s.at[h, 0], ag_r.at[h, 0], right),
            rcopy(red_own[h].at[every], red_r[h].at[every], ag_s.at[h, 1], ag_r.at[h, 1], left),
            rcopy(red_l[h].at[lo], red_o[h].at[lo], ag_s.at[h, 2], ag_r.at[h, 2], right),
            rcopy(red_r[h].at[hi], red_o[h].at[hi], ag_s.at[h, 3], ag_r.at[h, 3], left),
        )

    sum_gathers = [gathers(h) for h in range(2)]

    def start_gather(h):
        sum_gathers[h][0].start()
        sum_gathers[h][1].start()

    def forward_gather(h):
        sum_gathers[h][0].wait_recv()
        sum_gathers[h][2].start()
        sum_gathers[h][1].wait_recv()
        sum_gathers[h][3].start()

    HR = SH // 2
    up_, dn_ = pl.ds(0, HR), pl.ds(HR, HR)

    def root(s):
        return (
            rcopy(rraw.at[d, s], rraw.at[d, s], rt_s.at[s, 0], rt_r.at[s, 0], right),
            rcopy(rraw.at[d, s], rraw.at[d, s], rt_s.at[s, 1], rt_r.at[s, 1], left),
            rcopy(rraw.at[e3, s, up_], rraw.at[e3, s, up_], rt_s.at[s, 2], rt_r.at[s, 2], right),
            rcopy(rraw.at[e1, s, dn_], rraw.at[e1, s, dn_], rt_s.at[s, 3], rt_r.at[s, 3], left),
        )

    roots = [root(s) for s in range(S)]

    def start_root(s):
        roots[s][0].start()
        roots[s][1].start()

    def forward_root(s):
        roots[s][0].wait_recv()
        roots[s][2].start()
        roots[s][1].wait_recv()
        roots[s][3].start()

    def place(red, e, h):
        def one(q):
            for s in range(S):
                sb[s, q, rows(e), cols4(e, h)] = red[h][within(tab[0, q * S + s], N)]

        loop(F, one)

    def send_eighth(e, h):
        def one(i):
            q = peer(i + 1)
            rcopy(
                sb.at[:, q, rows(e), cols4(e, h)],
                gb.at[:, f, rows(e), cols4(e, h)],
                g_s.at[S], g_r.at[S], (d, q),
            ).start()

        loop(F - 1, one)

    def send_rest(s):
        def one(i):
            q = peer(i + 1)
            for r, c in ((rows(e3), cols4(e3, 1)), (rows(e1), cols4(e1, 1)), (rows(e2), cols(e2))):
                rcopy(sb.at[s, q, r, c], gb.at[s, f, r, c], g_s.at[s], g_r.at[s], (d, q)).start()

        loop(F - 1, one)

    def others(n):
        return pl.ds(0, n)

    ahead = rcopy(
        sb.at[:, others(F - 1), pl.ds(0, 16), :], gb.at[:, others(F - 1), pl.ds(0, 16), :],
        g_s.at[S], g_r.at[S], right,
    )
    rests = [
        rcopy(
            sb.at[s, others(F - 1), pl.ds(0, 16), :], gb.at[s, others(F - 1), pl.ds(0, 16), :],
            g_s.at[s], g_r.at[s], right,
        )
        for s in range(S)
    ]

    ld_g.wait()
    relay(0)
    for k in range(4):
        halves_of_sum[1][k].start()
    total(0)
    start_gather(0)
    place(red_own, d, 0)
    send_eighth(d, 0)
    relay(1)
    total(1)
    start_gather(1)
    place(red_own, d, 1)
    send_eighth(d, 1)
    forward_gather(0)
    place(red_l, e3, 0)
    send_eighth(e3, 0)
    place(red_r, e1, 0)
    send_eighth(e1, 0)
    forward_gather(1)
    start_root(0)
    start_root(1)
    place(red_l, e3, 1)
    place(red_r, e1, 1)
    for h in range(2):
        sum_gathers[h][2].wait_recv()
        sum_gathers[h][3].wait_recv()
        place(red_o, e2, h)
    selfs = [pltpu.make_async_copy(sb.at[s, f], gb.at[s, f], loc.at[4 + s]) for s in range(S)]
    send_rest(0)
    for s in range(S):
        selfs[s].start()
    send_rest(1)
    forward_root(0)
    start_root(2)
    ld_l.wait()
    ld_a.wait()

    def tile(j):
        return pl.ds(pl.multiple_of(j * T, T), T)

    def gcols(s, j):
        return gb[s, :, :, tile(j)].reshape(B, T)

    def grows(s, j):
        return gb[s, pl.ds(j * (T // 32), T // 32)].reshape(T, W)

    out_copies = {}

    def put(src, dst, k, s):
        cp = pltpu.make_async_copy(src, dst, outs.at[k, s])
        cp.start()
        out_copies[id(src)] = cp

    def free(src):
        cp = out_copies.pop(id(src), None)
        if cp is not None:
            cp.wait()

    def third(t):
        n = N // S
        own = pl.ds(t * n, n)
        a, b = pl.ds(t * n, n // 2), pl.ds(t * n + n // 2, n - n // 2)
        return (
            rcopy(uall.at[d, own], uall.at[d, own], u_s.at[t, 0], u_r.at[t, 0], right),
            rcopy(uall.at[d, own], uall.at[d, own], u_s.at[t, 1], u_r.at[t, 1], left),
            rcopy(uall.at[e3, a], uall.at[e3, a], u_s.at[t, 2], u_r.at[t, 2], right),
            rcopy(uall.at[e1, b], uall.at[e1, b], u_s.at[t, 3], u_r.at[t, 3], left),
        ) + tuple(
            rcopy(nall.at[d, own], nall.at[d, own], n_s.at[t, k], n_r.at[t, k], dev)
            for k, dev in enumerate((right, left, opp))
        )

    up_copies = [third(t) for t in range(S)]

    def shares(t):
        return rcopy(
            nls[t].at[others(F - 1)], nls[t].at[others(F - 1)], w_s.at[t], w_r.at[t], right
        )

    def start_third(t):
        rcopy(
            pb.at[t, others(F - 1)], us[t].at[others(F - 1)], p_s.at[t], p_r.at[t], right
        ).wait_recv()
        shares(t).wait_recv()

        def choose(i):
            j = t * (N // S) + i
            q, r = within(tab[1, j], F), tab[2, j]
            v = us[0][jnp.where(r == 0, q, F)].astype(F32)
            n = nls[0][jnp.where(r == 0, q, F)]
            for k in range(1, t + 1):
                v = v + us[k][jnp.where(r == k, q, F)].astype(F32)
                n = n + nls[k][jnp.where(r == k, q, F)]
            uall[d, j] = v.astype(BF)
            nall[d, j] = n

        loop(N // S, choose)
        for k in (0, 1, 4, 5, 6):
            up_copies[t][k].start()

    def forward_third(t):
        up_copies[t][0].wait_recv()
        up_copies[t][2].start()
        up_copies[t][1].wait_recv()
        up_copies[t][3].start()

    def statistics(s):
        free(ls)
        free(rs_)

        def left_stat(j):
            g = grows(s, j)
            ls[:, tile(j)] = dot_t(gmb[...], g).astype(BF)
            gct[:, tile(j)] = dot_t(sel[...], g).astype(BF)

        loop(NT, left_stat)
        put(ls, sl_out.at[s], 1, s)

        def right_stat(j):
            rs_[:, tile(j)] = dot(gct[...], gcols(s, j)).astype(BF)

        loop(NT, right_stat)
        put(rs_, sr_out.at[s], 2, s)

    def land_third(t):
        for k in (2, 3, 4, 5, 6):
            up_copies[t][k].wait_recv()
        own = pl.ds(t * (N // S), N // S)
        pairs = [(uall.at[e, own], up.at[own]) for e, up in enumerate((up_0, up_1, up_2, up_3))]
        for k, (src, dst) in enumerate(pairs + [(nall.at[:, own], nm_out.at[:, own])]):
            cp = pltpu.make_async_copy(src, dst, outs.at[4 + k, t])
            cp.start()
            landed.append(cp)

    landed = []
    tab_copy = pltpu.make_async_copy(tab_v, tab_out, outs.at[3, 0])
    tab_copy.start()
    ahead.wait_recv()
    for s in range(S):
        rests[s].wait_recv()
        selfs[s].wait()

        def halves(j):
            hf[:, tile(j)] = dot(lv[perm[s]], gcols(s, j)).astype(BF)

        loop(NT, halves)

        def mine(j, dn):
            g = dot(sel[...], gcols(s, j))
            gmb[:, tile(j)] = g.astype(BF)
            an = av[perm[s], :, tile(j)] + g * g
            anb[:, tile(j)] = an
            dr = g * lax.rsqrt(an)
            return dn + jnp.sum(dr * dr)

        free(anb)
        dn = lax.fori_loop(0, NT, mine, jnp.float32(0))
        put(anb, (an_0, an_1, an_2)[s], 0, s)

        if s + 1 < S:
            forward_root(s + 1)
        else:
            forward_third(0)
            statistics(s)
        roots[s][2].wait_recv()
        roots[s][3].wait_recv()

        def weave(t):
            part16 = pl.ds(pl.multiple_of(t * 16, 16), 16)
            quarter = [rraw[e, s, part16, :].astype(F32) for e in range(4)]
            for h in range(2):
                rows32 = jnp.concatenate([p[8 * h : 8 * h + 8] for p in quarter], axis=0)
                rn[pl.ds(pl.multiple_of(t * 64 + 32 * h, 32), 32), :] = rows32.astype(BF)

        loop(F // 2, weave)

        def prec(j, pn):
            p = dot(hf[...], rn[:, tile(j)])
            pv[:, tile(j)] = p
            return pn + jnp.sum(p * p)

        pn = lax.fori_loop(0, NT, prec, jnp.float32(0))

        lane = lax.broadcasted_iota(jnp.int32, (1, 128), 1)
        nb[s] = jnp.where(lane == 0, dn, jnp.where(lane == 1, pn, 0.0))

        def pack(q):
            v = pv[pl.ds(pl.multiple_of(q * 8, 8), 8), :]
            pb[s, q] = jnp.concatenate([v[:, :W2], v[:, W2:]], axis=0).astype(BF)

        loop(F, pack)
        us[s][f] = pb[s, f]
        nls[s][f] = nb[s]

        def send_p(i):
            q = peer(i + 1)
            rcopy(pb.at[s, q], us[s].at[f], p_s.at[s], p_r.at[s], (d, q)).start()
            rcopy(nb.at[s], nls[s].at[f], w_s.at[s], w_r.at[s], (d, q)).start()

        loop(F - 1, send_p)
        if s == 0:
            send_rest(2)
        if s == 1:
            start_third(0)
        if s + 1 < S:
            statistics(s)
        else:
            start_third(1)

    land_third(0)
    forward_third(1)
    start_third(2)
    land_third(1)
    forward_third(2)
    land_third(2)
    for h in range(2):
        for cp in halves_of_sum[h] + sum_gathers[h]:
            cp.wait_send()
    ahead.wait_send()
    for s in range(S):
        for cp in up_copies[s]:
            cp.wait_send()
        for cp in roots[s]:
            cp.wait_send()
        rests[s].wait_send()
        shares(s).wait_send()
        rcopy(pb.at[s, others(F - 1)], us[s].at[others(F - 1)], p_s.at[s], p_r.at[s], right).wait_send()
    for cp in landed + [tab_copy] + list(out_copies.values()):
        cp.wait()


def finish_kernel(nb, per, tab, *refs):
    ups, (nm, a0, a1, a2, sl, sr, left, right, up_o, left_o, right_o, acc_o) = refs[:4], refs[4:]
    step = pl.program_id(0)
    for b in range(nb):
        at = tab[4, step * nb + b]
        norms = nm[0, at] + nm[1, at] + nm[2, at] + nm[3, at]
        factor = jnp.sqrt(norms[:, 0:1] / (norms[:, 1:2] + 1e-06))
        parts = []
        for e in range(4):
            v = ups[e][at].astype(F32) * factor
            parts.append(jnp.concatenate([v[:8], v[8:]], axis=1))
        up_o[b] = jnp.concatenate(parts, axis=0).astype(BF)
    rank = jnp.full(acc_o.shape, tab[3, step // per], jnp.int32)
    acc_o[...] = jnp.where(rank == 0, a0[...], jnp.where(rank == 1, a1[...], a2[...]))
    left_o[...] = 0.95 * left[...] + 0.05 * sl[...].astype(F32)
    right_o[...] = 0.95 * right[...] + 0.05 * sr[...].astype(F32)


def body(grad_parts, left_stats, right_stats, accum, left_root, right_root, owner_slot):
    N = owner_slot.shape[0]
    F = lax.axis_size("fsdp")
    S = left_stats.shape[0]
    W = left_stats.shape[4]
    SH = F * 8
    H = N // 2
    W2 = W // 2
    hbm = pl.BlockSpec(memory_space=pl.ANY)
    vmem = pl.BlockSpec(memory_space=pltpu.VMEM)
    half = pltpu.VMEM((H, 16, W2), BF)
    whole = pltpu.VMEM((N + 1, 16, W // 4), BF)
    dma = pltpu.SemaphoreType.DMA
    share = jax.ShapeDtypeStruct((S, SH, W), BF)
    sl, sr, a0, a1, a2, up0, up1, up2, up3, nm, tab = pl.pallas_call(
        functools.partial(step_kernel, N, S, F, W),
        out_shape=(share, share) + (jax.ShapeDtypeStruct((SH, W), F32),) * 3
                  + (jax.ShapeDtypeStruct((N, 16, W2), BF),) * 4 + (
                   jax.ShapeDtypeStruct((4, N, 1, 128), F32),
                   jax.ShapeDtypeStruct((8, 128), jnp.int32)),
        in_specs=[vmem, hbm, hbm, hbm, hbm],
        out_specs=(hbm,) * 11,
        scratch_shapes=[pltpu.VMEM((N, 32, W), BF)]
        + [half] * 8
        + [whole] * 8
        + [
            pltpu.VMEM((S, F, 32, W), BF),
            pltpu.VMEM((S, F, 32, W), BF),
            pltpu.VMEM((4, S, SH, W), BF),
            pltpu.VMEM((F * 32, W), BF),
            pltpu.VMEM((S, SH, W), BF),
            pltpu.VMEM((S, SH, W), BF),
            pltpu.VMEM((S, SH, W), F32),
            pltpu.VMEM((SH, F * 32), BF),
            pltpu.VMEM((SH, W), BF),
            pltpu.VMEM((SH, W), F32),
            pltpu.VMEM((SH, F * 32), BF),
            pltpu.VMEM((SH, W), BF),
            pltpu.VMEM((SH, W), F32),
            pltpu.VMEM((SH, W), BF),
            pltpu.VMEM((SH, W), BF),
            pltpu.VMEM((S, F, 16, W2), BF),
            pltpu.VMEM((F + 1, 16, W2), BF),
            pltpu.VMEM((F + 1, 16, W2), BF),
            pltpu.VMEM((F + 1, 16, W2), BF),
            pltpu.VMEM((4, N, 16, W2), BF),
            pltpu.VMEM((S, 1, 128), F32),
            pltpu.VMEM((F + 1, 1, 128), F32),
            pltpu.VMEM((F + 1, 1, 128), F32),
            pltpu.VMEM((F + 1, 1, 128), F32),
            pltpu.VMEM((4, N, 1, 128), F32),
            pltpu.VMEM((8, 128), jnp.int32),
            pltpu.SMEM((8, 128), jnp.int32),
        ]
        + [
            dma((2, 6)), dma((2, 6)), dma((2, 4)), dma((2, 4)), dma((S, 4)), dma((S, 4)),
            dma((S + 1,)), dma((S + 1,)), dma((S,)), dma((S,)), dma((S,)), dma((S,)), dma((S, 3)), dma((S, 3)),
            dma((S, 4)), dma((S, 4)), dma((5 + S,)), dma((9, S)),
        ],
        compiler_params=pltpu.CompilerParams(
            collective_id=0, has_side_effects=True, vmem_limit_bytes=STEP_VMEM
        ),
        name="shampoo_step",
    )(
        owner_slot[None, :], grad_parts[0],
        left_root.reshape(S, SH, W), right_root.reshape(S, SH, W), accum.reshape(S, SH, W),
    )
    rows = S * SH
    K = 2 * S if N % (2 * S) == 0 and (rows // (2 * S)) % 16 == 0 else S
    nb, rb = N // K, rows // K
    per = K // S
    flat = pl.BlockSpec((rb, W), lambda i, tab: (i, 0))
    ranked = pl.BlockSpec((rb, W), lambda i, tab: (tab[3, i // per] * per + i % per, 0))
    one_rank = pl.BlockSpec((rb, W), lambda i, tab: (i % per, 0))

    def full(shape):
        return pl.BlockSpec(shape, lambda i, tab: (0,) * len(shape))

    stat = jax.ShapeDtypeStruct((rows, W), F32)
    update, left_out, right_out, accu_out = pl.pallas_call(
        functools.partial(finish_kernel, nb, per),
        grid_spec=pltpu.PrefetchScalarGridSpec(
            num_scalar_prefetch=1,
            grid=(K,),
            in_specs=[full((N, 16, W2))] * 4
            + [full((4, N, 1, 128))]
            + [one_rank] * 3
            + [ranked] * 2
            + [flat] * 2,
            out_specs=(pl.BlockSpec((nb, 32, W), lambda i, tab: (i, 0, 0)), flat, flat, flat),
        ),
        out_shape=(jax.ShapeDtypeStruct((N, 32, W), BF), stat, stat, stat),
        compiler_params=pltpu.CompilerParams(vmem_limit_bytes=FINISH_VMEM),
        name="shampoo_finish",
    )(
        tab, up0, up1, up2, up3, nm, a0, a1, a2, sl.reshape(rows, W), sr.reshape(rows, W),
        left_stats.reshape(rows, W), right_stats.reshape(rows, W),
    )
    layout = left_stats.shape
    return (update, left_out.reshape(layout), right_out.reshape(layout), accu_out.reshape(layout))


def solution(mesh):
    spread = P("fsdp", None, "dp", None, None)
    return jax.shard_map(
        body,
        mesh=mesh,
        in_specs=(P("dp", None, "fsdp", None),) + (spread,) * 5 + (P(),),
        out_specs=(P(None, "fsdp", None), spread, spread, spread),
        check_vma=False,
    )
```

time: 175 us -> 144 us (0.82)
  Pallas kernels: 173 us -> 143 us
    pallas_call x1, Pallas kernels: 159 us -> 137 us  [body(): pl.pallas_call(functools.partial(step_kernel, N, S, F, W), out_shape=(sha...]
    pallas_call x1, Pallas kernels: 14.4 us -> 5.8 us  [body(): pl.pallas_call(functools.partial(finish_kernel, nb, per), grid_spec=pltpu...]
where the time goes in v1:
time: 144 us
  Pallas kernels  143 us (99%)
    pallas_call x1, Pallas kernels, body(): pl.pallas_call(functools.partial(step_kernel, N, S, F, W), out_shape=(sha...  137 us
    pallas_call x1, Pallas kernels, body(): pl.pallas_call(functools.partial(finish_kernel, nb, per), grid_spec=pltpu...  5.8 us

profile of v1, /device:TPU:1, one launch (start us, length us, event | category | flops | bytes accessed | tf_op | source)
XLA Modules:
  0.0 144.0 jit_solution(15574074588989533336)
XLA Ops:
  0.6 0.0 copy-start.2
  0.6 0.6 copy-done.2
  1.3 0.0 copy-start
  1.3 0.0 copy-start.1
  1.3 136.9 %shampoo_step.1 = (bf16[3,256,1024]{2,1,0:T(8,128)(2,1)S(1)}, bf16[3,256,1024]{2,1,0:T(8,128)(2,1)S(1)}, f32[256,1024]{1,0:T(8,128)S(1)}, f32[256,1024]{1,0:T(8,...) custom-call(s32[1,36]{1,0:T(1,128)S(1)} %bitcast.22, ...), custom_call_target="tpu_custom_call" | custom-call | tf_op jit(solution)/shard_map/shampoo_step/pallas_call | solution.py:590
  138.2 0.0 copy-done
  138.2 0.0 copy-done.1
  138.2 5.8 %shampoo_finish.1 = (bf16[36,32,1024]{2,1,0:T(8,128)(2,1)}, f32[768,1024]{1,0:T(8,128)}, f32[768,1024]{1,0:T(8,128)}, f32[768,1024]{1,0:T(8,128)}) custom-call(s32[8,128]{1,0:T(8,128)S(1)} %get-tuple-element.19.tab, bf16[36,16,512]{2,1,0:T(8,128)(2,1)S(1)} %get-tuple-element.20.refs_0_, bf16[36,16,512]{2,1,0:T(8,128)(2,1)S(1)} %get-tuple-element.21.refs_1_, ...), custom_call_target="tpu_custom_call" | custom-call | tf_op jit(solution)/shard_map/shampoo_finish/pallas_call | solution.py:655
Async XLA Ops:
  0.6 0.7 copy-start.2
  1.3 136.9 %copy-start = (f32[3,32,1,8,1024]{4,3,2,1,0:T(8,128)S(1)}, f32[3,32,1,8,1024]{4,3,2,1,0:T(8,128)}, u32[]{:S(2)}) copy-start(f32[3,32,1,8,1024]{4,3,2,1,0:T(8,128)} %param.8) | copy-start | bytes 9437188
  1.3 136.9 %copy-start.1 = (f32[3,32,1,8,1024]{4,3,2,1,0:T(8,128)S(1)}, f32[3,32,1,8,1024]{4,3,2,1,0:T(8,128)}, u32[]{:S(2)}) copy-start(f32[3,32,1,8,1024]{4,3,2,1,0:T(8,128)} %param.9) | copy-start | bytes 9437188

commit v2 on v1

--- a/solution.py
+++ b/solution.py
@@ -77,7 +77,9 @@
     def part(h):
         return pl.ds(h * W4, W4)
 
-    def loop(n, fn, unroll=1):
+    def loop(n, fn, unroll=4):
+        unroll = n if n == F - 1 else unroll
+        unroll = unroll if n % unroll == 0 else 1
         lax.fori_loop(0, n, lambda i, _: (fn(i), 0)[1], 0, unroll=unroll)
 
     ld_g = pltpu.make_async_copy(gp_in, gp, loc.at[4 + S])
@@ -99,17 +101,6 @@
     loop(F - 1, greet)
     red_own, red_l = (red_own_0, red_own_1), (red_l_0, red_l_1)
     red_r, red_o = (red_r_0, red_r_1), (red_o_0, red_o_1)
-    for ref in red_own + red_l + red_r + red_o:
-        ref[N] = jnp.zeros((16, W4), BF)
-    us = (u_0, u_1, u_2)
-    for ref in us:
-        ref[F] = jnp.zeros((16, W2), BF)
-    nls = (nl_0, nl_1, nl_2)
-    for ref in nls:
-        ref[F] = jnp.zeros((1, 128), F32)
-    pick = lax.broadcasted_iota(jnp.int32, (SH, B), 0)
-    at = lax.broadcasted_iota(jnp.int32, (SH, B), 1)
-    sel[...] = jnp.where(at == (pick // 8) * 32 + d * 8 + pick % 8, 1.0, 0.0).astype(BF)
     pl.semaphore_wait(barrier, F + 2)
 
     def tables():
@@ -181,7 +172,7 @@
         def add_a(b):
             ca[b, :, p] = (ra[b, :, p].astype(F32) + gp[b, rows(e1), cols4(e1, h)].astype(F32)).astype(BF)
 
-        loop(H, add_a)
+        loop(H, add_a, 3)
         c[4].start()
         c[1].wait_recv()
 
@@ -190,7 +181,7 @@
                 rb[b, :, p].astype(F32) + gp[H + b, rows(e3), cols4(e3, h)].astype(F32)
             ).astype(BF)
 
-        loop(H, add_b)
+        loop(H, add_b, 3)
         c[5].start()
 
     def total(h):
@@ -204,7 +195,7 @@
                 own + fa_raw[b, :, p].astype(F32) + fa_comb[b, :, p].astype(F32)
             ).astype(BF)
 
-        loop(H, fin_a)
+        loop(H, fin_a, 3)
         c[2].wait_recv()
         c[5].wait_recv()
 
@@ -214,11 +205,113 @@
                 own + fb_raw[b, :, p].astype(F32) + fb_comb[b, :, p].astype(F32)
             ).astype(BF)
 
-        loop(H, fin_b)
+        loop(H, fin_b, 3)
 
     halves_of_sum = [sums(h) for h in range(2)]
     for k in range(4):
         halves_of_sum[0][k].start()
+
+    every = pl.ds(0, N)
+
+    def gathers(h):
+        return (
+            rcopy(red_own[h].at[every], red_l[h].at[every], ag_s.at[h, 0], ag_r.at[h, 0], right),
+            rcopy(red_own[h].at[every], red_r[h].at[every], ag_s.at[h, 1], ag_r.at[h, 1], left),
+            rcopy(red_l[h].at[lo], red_o[h].at[lo], ag_s.at[h, 2], ag_r.at[h, 2], right),
+            rcopy(red_r[h].at[hi], red_o[h].at[hi], ag_s.at[h, 3], ag_r.at[h, 3], left),
+        )
+
+    sum_gathers = [gathers(h) for h in range(2)]
+
+    def start_gather(h):
+        sum_gathers[h][0].start()
+        sum_gathers[h][1].start()
+
+    def forward_gather(h):
+        sum_gathers[h][0].wait_recv()
+        sum_gathers[h][2].start()
+        sum_gathers[h][1].wait_recv()
+        sum_gathers[h][3].start()
+
+    HR = SH // 2
+    up_, dn_ = pl.ds(0, HR), pl.ds(HR, HR)
+
+    def root(s):
+        return (
+            rcopy(rraw.at[d, s], rraw.at[d, s], rt_s.at[s, 0], rt_r.at[s, 0], right),
+            rcopy(rraw.at[d, s], rraw.at[d, s], rt_s.at[s, 1], rt_r.at[s, 1], left),
+            rcopy(rraw.at[e3, s, up_], rraw.at[e3, s, up_], rt_s.at[s, 2], rt_r.at[s, 2], right),
+            rcopy(rraw.at[e1, s, dn_], rraw.at[e1, s, dn_], rt_s.at[s, 3], rt_r.at[s, 3], left),
+        )
+
+    roots = [root(s) for s in range(S)]
+
+    def start_root(s):
+        roots[s][0].start()
+        roots[s][1].start()
+
+    def forward_root(s):
+        roots[s][0].wait_recv()
+        roots[s][2].start()
+        roots[s][1].wait_recv()
+        roots[s][3].start()
+
+    def place(red, e, h):
+        def one(q):
+            for s in range(S):
+                sb[s, q, rows(e), cols4(e, h)] = red[h][within(tab[0, q * S + s], N)]
+
+        loop(F, one)
+
+    def send_eighth(e, h):
+        def one(i):
+            q = peer(i + 1)
+            rcopy(
+                sb.at[:, q, rows(e), cols4(e, h)],
+                gb.at[:, f, rows(e), cols4(e, h)],
+                g_s.at[S], g_r.at[S], (d, q),
+            ).start()
+
+        loop(F - 1, one)
+
+    def send_rest(s):
+        def one(i):
+            q = peer(i + 1)
+            for r, c in ((rows(e3), cols4(e3, 1)), (rows(e1), cols4(e1, 1)), (rows(e2), cols(e2))):
+                rcopy(sb.at[s, q, r, c], gb.at[s, f, r, c], g_s.at[s], g_r.at[s], (d, q)).start()
+
+        loop(F - 1, one)
+
+    def others(n):
+        return pl.ds(0, n)
+
+    ahead = rcopy(
+        sb.at[:, others(F - 1), pl.ds(0, 16), :], gb.at[:, others(F - 1), pl.ds(0, 16), :],
+        g_s.at[S], g_r.at[S], right,
+    )
+    rests = [
+        rcopy(
+            sb.at[s, others(F - 1), pl.ds(0, 16), :], gb.at[s, others(F - 1), pl.ds(0, 16), :],
+            g_s.at[s], g_r.at[s], right,
+        )
+        for s in range(S)
+    ]
+
+    ld_g.wait()
+    relay(0)
+    for k in range(4):
+        halves_of_sum[1][k].start()
+    for ref in red_own + red_l + red_r + red_o:
+        ref[N] = jnp.zeros((16, W4), BF)
+    us = (u_0, u_1, u_2)
+    for ref in us:
+        ref[F] = jnp.zeros((16, W2), BF)
+    nls = (nl_0, nl_1, nl_2)
+    for ref in nls:
+        ref[F] = jnp.zeros((1, 128), F32)
+    pick = lax.broadcasted_iota(jnp.int32, (SH, B), 0)
+    at = lax.broadcasted_iota(jnp.int32, (SH, B), 1)
+    sel[...] = jnp.where(at == (pick // 8) * 32 + d * 8 + pick % 8, 1.0, 0.0).astype(BF)
     tables()
     to_scalars = pltpu.make_async_copy(tab_v, tab, loc.at[3])
     to_scalars.start()
@@ -229,105 +322,6 @@
         for s in range(1, S):
             k = jnp.where(tab[3, s] == r, s, k)
         perm.append(within(k, S - 1))
-    ld_r.wait()
-
-    def reorder(t):
-        part = pl.ds(pl.multiple_of(t * 16, 16), 16)
-        for r in range(S):
-            rraw[d, r, part, :] = rv[perm[r], part, :]
-
-    loop(SH // 16, reorder)
-
-    every = pl.ds(0, N)
-
-    def gathers(h):
-        return (
-            rcopy(red_own[h].at[every], red_l[h].at[every], ag_s.at[h, 0], ag_r.at[h, 0], right),
-            rcopy(red_own[h].at[every], red_r[h].at[every], ag_s.at[h, 1], ag_r.at[h, 1], left),
-            rcopy(red_l[h].at[lo], red_o[h].at[lo], ag_s.at[h, 2], ag_r.at[h, 2], right),
-            rcopy(red_r[h].at[hi], red_o[h].at[hi], ag_s.at[h, 3], ag_r.at[h, 3], left),
-        )
-
-    sum_gathers = [gathers(h) for h in range(2)]
-
-    def start_gather(h):
-        sum_gathers[h][0].start()
-        sum_gathers[h][1].start()
-
-    def forward_gather(h):
-        sum_gathers[h][0].wait_recv()
-        sum_gathers[h][2].start()
-        sum_gathers[h][1].wait_recv()
-        sum_gathers[h][3].start()
-
-    HR = SH // 2
-    up_, dn_ = pl.ds(0, HR), pl.ds(HR, HR)
-
-    def root(s):
-        return (
-            rcopy(rraw.at[d, s], rraw.at[d, s], rt_s.at[s, 0], rt_r.at[s, 0], right),
-            rcopy(rraw.at[d, s], rraw.at[d, s], rt_s.at[s, 1], rt_r.at[s, 1], left),
-            rcopy(rraw.at[e3, s, up_], rraw.at[e3, s, up_], rt_s.at[s, 2], rt_r.at[s, 2], right),
-            rcopy(rraw.at[e1, s, dn_], rraw.at[e1, s, dn_], rt_s.at[s, 3], rt_r.at[s, 3], left),
-        )
-
-    roots = [root(s) for s in range(S)]
-
-    def start_root(s):
-        roots[s][0].start()
-        roots[s][1].start()
-
-    def forward_root(s):
-        roots[s][0].wait_recv()
-        roots[s][2].start()
-        roots[s][1].wait_recv()
-        roots[s][3].start()
-
-    def place(red, e, h):
-        def one(q):
-            for s in range(S):
-                sb[s, q, rows(e), cols4(e, h)] = red[h][within(tab[0, q * S + s], N)]
-
-        loop(F, one)
-
-    def send_eighth(e, h):
-        def one(i):
-            q = peer(i + 1)
-            rcopy(
-                sb.at[:, q, rows(e), cols4(e, h)],
-                gb.at[:, f, rows(e), cols4(e, h)],
-                g_s.at[S], g_r.at[S], (d, q),
-            ).start()
-
-        loop(F - 1, one)
-
-    def send_rest(s):
-        def one(i):
-            q = peer(i + 1)
-            for r, c in ((rows(e3), cols4(e3, 1)), (rows(e1), cols4(e1, 1)), (rows(e2), cols(e2))):
-                rcopy(sb.at[s, q, r, c], gb.at[s, f, r, c], g_s.at[s], g_r.at[s], (d, q)).start()
-
-        loop(F - 1, one)
-
-    def others(n):
-        return pl.ds(0, n)
-
-    ahead = rcopy(
-        sb.at[:, others(F - 1), pl.ds(0, 16), :], gb.at[:, others(F - 1), pl.ds(0, 16), :],
-        g_s.at[S], g_r.at[S], right,
-    )
-    rests = [
-        rcopy(
-            sb.at[s, others(F - 1), pl.ds(0, 16), :], gb.at[s, others(F - 1), pl.ds(0, 16), :],
-            g_s.at[s], g_r.at[s], right,
-        )
-        for s in range(S)
-    ]
-
-    ld_g.wait()
-    relay(0)
-    for k in range(4):
-        halves_of_sum[1][k].start()
     total(0)
     start_gather(0)
     place(red_own, d, 0)
@@ -337,6 +331,14 @@
     start_gather(1)
     place(red_own, d, 1)
     send_eighth(d, 1)
+    ld_r.wait()
+
+    def reorder(t):
+        part = pl.ds(pl.multiple_of(t * 16, 16), 16)
+        for r in range(S):
+            rraw[d, r, part, :] = rv[perm[r], part, :]
+
+    loop(SH // 16, reorder)
     forward_gather(0)
     place(red_l, e3, 0)
     send_eighth(e3, 0)
@@ -439,13 +441,13 @@
             ls[:, tile(j)] = dot_t(gmb[...], g).astype(BF)
             gct[:, tile(j)] = dot_t(sel[...], g).astype(BF)
 
-        loop(NT, left_stat)
+        loop(NT, left_stat, 1)
         put(ls, sl_out.at[s], 1, s)
 
         def right_stat(j):
             rs_[:, tile(j)] = dot(gct[...], gcols(s, j)).astype(BF)
 
-        loop(NT, right_stat)
+        loop(NT, right_stat, 1)
         put(rs_, sr_out.at[s], 2, s)
 
     def land_third(t):
@@ -469,7 +471,7 @@
         def halves(j):
             hf[:, tile(j)] = dot(lv[perm[s]], gcols(s, j)).astype(BF)
 
-        loop(NT, halves)
+        loop(NT, halves, 1)
 
         def mine(j, dn):
             g = dot(sel[...], gcols(s, j))

time: 144 us -> 142 us (0.986)
  Pallas kernels: 143 us -> 140 us
    pallas_call x1, Pallas kernels: 137 us -> 134 us  [body(): pl.pallas_call(functools.partial(step_kernel, N, S, F, W), out_shape=(sha...]
where the time goes in v2:
time: 142 us; the launch traced here: 141 us
  Pallas kernels  140 us (99%)
    pallas_call x1, Pallas kernels, body(): pl.pallas_call(functools.partial(step_kernel, N, S, F, W), out_shape=(sha...  134 us
    pallas_call x1, Pallas kernels, body(): pl.pallas_call(functools.partial(finish_kernel, nb, per), grid_spec=pltpu...  5.8 us

profile of v2, /device:TPU:1, one launch (start us, length us, event | category | flops | bytes accessed | tf_op | source)
XLA Modules:
  0.0 141.1 jit_solution(4822592130834378110)
XLA Ops:
  0.6 0.0 copy-start.2
  0.6 0.6 copy-done.2
  1.3 0.0 copy-start
  1.3 0.0 copy-start.1
  1.3 134.0 %shampoo_step.1 = (bf16[3,256,1024]{2,1,0:T(8,128)(2,1)S(1)}, bf16[3,256,1024]{2,1,0:T(8,128)(2,1)S(1)}, f32[256,1024]{1,0:T(8,128)S(1)}, f32[256,1024]{1,0:T(8,...) custom-call(s32[1,36]{1,0:T(1,128)S(1)} %bitcast.22, ...), custom_call_target="tpu_custom_call" | custom-call | tf_op jit(solution)/shard_map/shampoo_step/pallas_call | solution.py:592
  135.3 0.0 copy-done
  135.3 0.0 copy-done.1
  135.3 5.8 %shampoo_finish.1 = (bf16[36,32,1024]{2,1,0:T(8,128)(2,1)}, f32[768,1024]{1,0:T(8,128)}, f32[768,1024]{1,0:T(8,128)}, f32[768,1024]{1,0:T(8,128)}) custom-call(s32[8,128]{1,0:T(8,128)S(1)} %get-tuple-element.19.tab, bf16[36,16,512]{2,1,0:T(8,128)(2,1)S(1)} %get-tuple-element.20.refs_0_, bf16[36,16,512]{2,1,0:T(8,128)(2,1)S(1)} %get-tuple-element.21.refs_1_, ...), custom_call_target="tpu_custom_call" | custom-call | tf_op jit(solution)/shard_map/shampoo_finish/pallas_call | solution.py:657
Async XLA Ops:
  0.6 0.7 copy-start.2
  1.3 134.0 %copy-start = (f32[3,32,1,8,1024]{4,3,2,1,0:T(8,128)S(1)}, f32[3,32,1,8,1024]{4,3,2,1,0:T(8,128)}, u32[]{:S(2)}) copy-start(f32[3,32,1,8,1024]{4,3,2,1,0:T(8,128)} %param.8) | copy-start | bytes 9437188
  1.3 134.0 %copy-start.1 = (f32[3,32,1,8,1024]{4,3,2,1,0:T(8,128)S(1)}, f32[3,32,1,8,1024]{4,3,2,1,0:T(8,128)}, u32[]{:S(2)}) copy-start(f32[3,32,1,8,1024]{4,3,2,1,0:T(8,128)} %param.9) | copy-start | bytes 9437188

commit v3 on v2

--- a/solution.py
+++ b/solution.py
@@ -441,13 +441,13 @@
             ls[:, tile(j)] = dot_t(gmb[...], g).astype(BF)
             gct[:, tile(j)] = dot_t(sel[...], g).astype(BF)
 
-        loop(NT, left_stat, 1)
+        loop(NT, left_stat, 4)
         put(ls, sl_out.at[s], 1, s)
 
         def right_stat(j):
             rs_[:, tile(j)] = dot(gct[...], gcols(s, j)).astype(BF)
 
-        loop(NT, right_stat, 1)
+        loop(NT, right_stat, 4)
         put(rs_, sr_out.at[s], 2, s)
 
     def land_third(t):
@@ -471,7 +471,7 @@
         def halves(j):
             hf[:, tile(j)] = dot(lv[perm[s]], gcols(s, j)).astype(BF)
 
-        loop(NT, halves, 1)
+        loop(NT, halves, 4)
 
         def mine(j, dn):
             g = dot(sel[...], gcols(s, j))
@@ -482,7 +482,7 @@
             return dn + jnp.sum(dr * dr)
 
         free(anb)
-        dn = lax.fori_loop(0, NT, mine, jnp.float32(0))
+        dn = lax.fori_loop(0, NT, mine, jnp.float32(0), unroll=NT)
         put(anb, (an_0, an_1, an_2)[s], 0, s)
 
         if s + 1 < S:
@@ -507,7 +507,7 @@
             pv[:, tile(j)] = p
             return pn + jnp.sum(p * p)
 
-        pn = lax.fori_loop(0, NT, prec, jnp.float32(0))
+        pn = lax.fori_loop(0, NT, prec, jnp.float32(0), unroll=NT)
 
         lane = lax.broadcasted_iota(jnp.int32, (1, 128), 1)
         nb[s] = jnp.where(lane == 0, dn, jnp.where(lane == 1, pn, 0.0))

time: 142 us -> 139 us (0.979)
  Pallas kernels: 140 us -> 136 us
    pallas_call x1, Pallas kernels: 134 us -> 130 us  [body(): pl.pallas_call(functools.partial(step_kernel, N, S, F, W), out_shape=(sha...]
where the time goes in v3:
time: 139 us; the launch traced here: 137 us
  Pallas kernels  136 us (98%)
    pallas_call x1, Pallas kernels, body(): pl.pallas_call(functools.partial(step_kernel, N, S, F, W), out_shape=(sha...  130 us
    pallas_call x1, Pallas kernels, body(): pl.pallas_call(functools.partial(finish_kernel, nb, per), grid_spec=pltpu...  5.8 us

profile of v3, /device:TPU:1, one launch (start us, length us, event | category | flops | bytes accessed | tf_op | source)
XLA Modules:
  0.0 137.0 jit_solution(10638395749318955146)
XLA Ops:
  0.6 0.0 copy-start.2
  0.6 0.6 copy-done.2
  1.3 0.0 copy-start
  1.3 0.0 copy-start.1
  1.3 129.8 %shampoo_step.1 = (bf16[3,256,1024]{2,1,0:T(8,128)(2,1)S(1)}, bf16[3,256,1024]{2,1,0:T(8,128)(2,1)S(1)}, f32[256,1024]{1,0:T(8,128)S(1)}, f32[256,1024]{1,0:T(8,...) custom-call(s32[1,36]{1,0:T(1,128)S(1)} %bitcast.22, ...), custom_call_target="tpu_custom_call" | custom-call | tf_op jit(solution)/shard_map/shampoo_step/pallas_call | solution.py:592
  131.2 0.0 copy-done
  131.2 0.0 copy-done.1
  131.2 5.8 %shampoo_finish.1 = (bf16[36,32,1024]{2,1,0:T(8,128)(2,1)}, f32[768,1024]{1,0:T(8,128)}, f32[768,1024]{1,0:T(8,128)}, f32[768,1024]{1,0:T(8,128)}) custom-call(s32[8,128]{1,0:T(8,128)S(1)} %get-tuple-element.19.tab, bf16[36,16,512]{2,1,0:T(8,128)(2,1)S(1)} %get-tuple-element.20.refs_0_, bf16[36,16,512]{2,1,0:T(8,128)(2,1)S(1)} %get-tuple-element.21.refs_1_, ...), custom_call_target="tpu_custom_call" | custom-call | tf_op jit(solution)/shard_map/shampoo_finish/pallas_call | solution.py:657
Async XLA Ops:
  0.6 0.7 copy-start.2
  1.3 129.9 %copy-start = (f32[3,32,1,8,1024]{4,3,2,1,0:T(8,128)S(1)}, f32[3,32,1,8,1024]{4,3,2,1,0:T(8,128)}, u32[]{:S(2)}) copy-start(f32[3,32,1,8,1024]{4,3,2,1,0:T(8,128)} %param.8) | copy-start | bytes 9437188
  1.3 129.9 %copy-start.1 = (f32[3,32,1,8,1024]{4,3,2,1,0:T(8,128)S(1)}, f32[3,32,1,8,1024]{4,3,2,1,0:T(8,128)}, u32[]{:S(2)}) copy-start(f32[3,32,1,8,1024]{4,3,2,1,0:T(8,128)} %param.9) | copy-start | bytes 9437188
